TPU v7x, 32 devices: a whole 2x2x4 slice. The times are simulated.
32 devices in a mesh: groups: 2 (over x), det: 16 (over z, y, core).
Axes of the slice: x: 2, y: 2, z: 4, core: 2. Of those that a mesh axis runs over, the one named last changes fastest.
Arguments:
- timestream: float32 [2048, 4096], P(('groups', 'det')), parts along dimension 0, may hold values from -31 to 31
- seg_gains: float32 [2048, 4], P(('groups', 'det')), parts along dimension 0, may hold values from 0.25 to 1.75
- seg_bounds: int32 [2048, 3], P(('groups', 'det')), parts along dimension 0, may hold values from 512 to 3584, as said below
- det_band: int32 [2048], P(('groups', 'det')), parts along dimension 0, may hold values from 0 to 1
- band_taps: float32 [2, 32], replicated, may hold values from -1 to 1
- det_wafer: int32 [2048], P(('groups', 'det')), parts along dimension 0, may hold values from 0 to 7, as said below
- wafer_modes: float32 [16, 4096], P('groups'), parts along dimension 0, may hold values from -4 to 4
Outputs:
- covariance: float32 [2048, 1024], P(('groups', 'det')), parts along dimension 0
There are 2 independent parts, one for each index of `groups`. A program takes and returns all parts, laid end to end along the dimension named above; an argument that names none is the same for every part. Nothing has to cross between parts.
Inputs may be any that keep to these rules, and one draw needn't show every extreme that they name: `seg_bounds`: each detector's boundaries rise strictly. `det_wafer`: every wafer has detectors.
All inputs are finite; a program needn't handle non-finite values.
Results may differ from a plain program's by a relative error of at most 0.00086.
Values may be sent and summed in bfloat16 or wider, within the bound.
A program may use at most 128 MiB of HBM per device.

v0:
```python
import jax
import jax.numpy as jnp
from jax import lax
from jax.sharding import PartitionSpec as P


def filter_rows(timestream, seg_gains, seg_bounds, det_band, band_taps):
    det_rows = timestream.shape[0]
    samples = timestream.shape[1]
    tap_count = band_taps.shape[1]
    moments = jnp.arange(samples, dtype=jnp.int32)
    segment = jnp.zeros((det_rows, samples), jnp.int32)
    for column in range(seg_bounds.shape[1]):
        segment = segment + (moments[None, :] >= seg_bounds[:, column : column + 1]).astype(
            jnp.int32
        )
    profile = jnp.zeros((det_rows, samples), jnp.float32)
    for column in range(seg_gains.shape[1]):
        profile = profile + jnp.where(segment == column, seg_gains[:, column : column + 1], 0.0)
    scaled = timestream * profile
    own_taps = jnp.zeros((det_rows, tap_count), jnp.float32)
    for band_index in range(band_taps.shape[0]):
        own_taps = own_taps + jnp.where(
            det_band[:, None] == band_index, band_taps[band_index][None, :], 0.0
        )
    padded = jnp.pad(scaled, ((0, 0), (tap_count - 1, 0)))
    kernel = own_taps[:, ::-1][:, None, :]
    result = lax.conv_general_dilated(
        padded[None],
        kernel,
        (1,),
        "VALID",
        dimension_numbers=("NCH", "OIH", "NCH"),
        feature_group_count=det_rows,
        precision=lax.Precision.HIGHEST,
    )
    return result[0]


def project(filtered, det_wafer, wafer_modes):
    onehot = (
        det_wafer[:, None] == jnp.arange(wafer_modes.shape[0], dtype=jnp.int32)[None, :]
    ).astype(jnp.float32)
    own_mode = jnp.dot(onehot, wafer_modes, precision=lax.Precision.HIGHEST)
    coupling = jnp.mean(filtered * own_mode, axis=1, keepdims=True) / (
        jnp.mean(own_mode * own_mode, axis=1, keepdims=True) + 1e-06
    )
    return (filtered - coupling * own_mode).astype(jnp.bfloat16)


def pair_block(left_rows, right_rows):
    return lax.dot_general(
        left_rows, right_rows, (((1,), (1,)), ((), ())), preferred_element_type=jnp.float32
    )


def on_device(timestream, seg_gains, seg_bounds, det_band, band_taps, det_wafer, wafer_modes):
    cleaned = project(
        filter_rows(timestream, seg_gains, seg_bounds, det_band, band_taps), det_wafer, wafer_modes
    )
    det_rows = cleaned.shape[0]
    samples = cleaned.shape[1]
    devices = lax.axis_size("det")
    widened = cleaned.astype(jnp.float32)
    mean_power = lax.psum(jnp.sum(widened * widened), "det") / (det_rows * devices * samples)
    covar = pair_block(cleaned, lax.all_gather(cleaned, "det", axis=0, tiled=True))
    return covar / (samples * mean_power)


def solution(mesh):
    return jax.shard_map(
        on_device,
        mesh=mesh,
        in_specs=(
            P(("groups", "det"), None),
            P(("groups", "det"), None),
            P(("groups", "det"), None),
            P(("groups", "det")),
            P(),
            P(("groups", "det")),
            P("groups", None),
        ),
        out_specs=P(("groups", "det"), None),
        check_vma=False,
    )
```

profile of v0, /device:TPU:0, one launch (start us, length us, event | category | flops | bytes accessed | tf_op | source)
XLA Modules:
  0.0 120.2 jit_solution(17536795281282018858)
XLA Ops:
  6.5 0.0 copy-start
  6.5 0.0 all-gather.2.cloned.1.call-start
  6.5 0.7 broadcast_compare_fusion.1
  7.2 0.8 slice_bitcast_fusion.2
  8.0 0.8 slice_bitcast_fusion.9
  8.8 0.8 slice_bitcast_fusion.6
  9.6 0.1 select_add_fusion
  9.7 0.6 rev.3
  10.3 2.1 %add_multiply_fusion = f32[64,4096]{1,0:T(8,128)S(1)} fusion(f32[64,4096]{1,0:T(8,128)} %param.7, f32[64]{0:T(128)S(1)} %get-tuple-element.14, f32[64]{0:T(128)S(1)} %get-tuple-element.15, f32[64]{0:T(128)S(1)} %get-tuple-element.13, f32[64]{0:T(128)S(1)} %get-tuple-element.12, s32[64]{0:T(128)S(1)} %get-tuple-element.10, s32[64]{0:T(128)S(1)} %get-tuple-element.11, ...), kind=kLoop, calls=%fused_computation.16 | loop fusion | flops 5242880 | bytes 2098944 | tf_op jit(solution)/shard_map/mul | solution.py:20
  12.4 0.3 pad_bitcast_fusion
  12.8 0.1 pad.5
  12.8 0.7 reshape.19
  13.6 1.3 %copy.9 = f32[64,1,8,516]{0,2,3,1:T(8,128)S(1)} copy(f32[64,1,8,516]{3,2,0,1:T(8,128)S(1)} %reshape.19) | data formatting | bytes 2113536 | tf_op jit(solution)/shard_map/conv_general_dilated | solution.py:28
  14.9 8.2 %fusion.5 = f32[8,516,64]{2,0,1:T(8,128)} fusion(f32[64,1,32]{0,1,2:T(1,128)} %bitcast.43, f32[64,1,7,31]{0,2,3,1:T(8,128)S(1)} %slice.38, f32[64,1,8,516]{0,2,3,1:T(8,128)S(1)} %copy.9, pred[8,516]{0,1:T(8,128)(4,1)} %constant.33), kind=kOutput, calls=%fused_computation.6 | convolution fusion | flops 102554112 | bytes 2181408 | tf_op jit(solution)/shard_map/conv_general_dilated | solution.py:28
  23.1 0.0 copy-start.1
  23.1 2.5 %copy.10 = f32[8,516,64]{1,0,2:T(8,128)S(1)} copy(f32[8,516,64]{2,0,1:T(8,128)} %fusion.5) | data formatting | bytes 2113536 | tf_op jit(solution)/shard_map/conv_general_dilated | solution.py:28
  25.6 0.4 reshape.23
  25.9 0.0 copy-done
  26.0 0.0 copy-done.1
  26.0 0.8 multiply_reduce_fusion.2
  26.8 1.7 %multiply_reduce_fusion = (f32[]{:T(128)}, bf16[64,4096]{1,0:T(8,128)(2,1)}) fusion(f32[64,4096]{1,0:T(8,128)S(1)} %get-tuple-element.20, f32[64]{0:T(128)S(1)} %add_divide_fusion, f32[1,4128,64]{1,2,0:T(8,128)S(1)} %reshape.23), kind=kLoop, calls=%fused_computation.12 | loop fusion | flops 1572863 | bytes 2621700 | tf_op jit(solution)/shard_map/reduce_sum | solution.py:65
  28.4 0.0 all-gather.2.cloned.1.call-update
  28.5 36.2 %psum.7 = f32[]{:T(128)} all-reduce(f32[]{:T(128)} %get-tuple-element.7), channel_id=1, replica_groups=mesh['groups'=2,'det'=16] {'det'}, use_global_device_ids=true, to_apply=%region_3.4 | all-reduce | flops 1 | bytes 8 | tf_op jit(solution)/shard_map/psum | solution.py:65
  65.3 41.1 %all-gather.2.cloned.1.call-done = bf16[1024,4096]{1,0:T(8,128)(2,1)} async-done(((bf16[64,4096]{1,0:T(8,128)(2,1)}), bf16[1024,4096]{1,0:T(8,128)(2,1)}) %all-gather.2.cloned.1.call-update) | async-done | bytes 8388624 | tf_op jit(solution)/shard_map/all_gather | solution.py:66
  106.4 6.9 %convolution_divide_fusion = f32[64,1024]{1,0:T(8,128)} fusion(bf16[64,4096]{1,0:T(8,128)(2,1)} %get-tuple-element.8, bf16[1024,4096]{1,0:T(8,128)(2,1)} %all-gather.2.cloned.1.call-done, f32[]{:T(128)S(6)} %mul.29), kind=kOutput, calls=%fused_computation.7 | convolution fusion | flops 536936448 | bytes 9175044 | tf_op jit(solution)/shard_map/dot_general | solution.py:52
  (2 shorter events, 0.0 us)
Async XLA Ops:
  6.5 19.4 %copy-start = (f32[8,4096]{1,0:T(8,128)S(1)}, f32[8,4096]{1,0:T(8,128)}, u32[]{:S(2)}) copy-start(f32[8,4096]{1,0:T(8,128)} %param.13) | copy-start | bytes 393220
  6.5 99.9 %all-gather.2.cloned.1.call-start = ((), (), s32[]{:S(2)}) async-start(), calls=%async_computation | async-start | bytes 8912896 | tf_op jit(solution)/shard_map/all_gather | solution.py:66
  23.1 2.9 %copy-start.1 = (s32[64]{0:T(128)S(1)}, s32[64]{0:T(128)}, u32[]{:S(2)}) copy-start(s32[64]{0:T(128)} %param.12) | copy-start | bytes 772
Sparse Core Ops, SparseCore 0:
  28.6 77.7 all-gather.1
where the time goes:
time: 121 us; the launch traced here: 120 us
  waiting for transfers between devices  41.1 us (34%)
  blocking collectives  36.2 us (30%)
  matrix products  15.9 us (13%)
  between operations  14.1 us (12%)
  local copies, waits for them, and re-layouts  8.31 us (7%)
  other arithmetic  4.54 us (4%)
    all_gather x1, waiting for transfers between devices, on_device(): lax.all_gather(cleaned, 'det', axis=0, tiled=True)  41.1 us
    psum x1, blocking collectives, on_device(): lax.psum(jnp.sum(widened * widened), 'det') / (det_rows * devices * samples)  36.2 us
    conv_general_dilated x1, matrix products, filter_rows(): lax.conv_general_dilated(padded[None], kernel, (1,), 'VALID', dimension_n...  8.17 us
    dot_general x1, matrix products, pair_block(): lax.dot_general(left_rows, right_rows, (((1,), (1,)), ((), ())), preferre...  6.93 us
    conv_general_dilated x5, local copies, waits for them, and re-layouts, filter_rows(): lax.conv_general_dilated(padded[None], kernel, (1,), 'VALID', dimension_n...  4.88 us
  transfers between devices with their start and end apart: 1, of which 1 were waited for; matrix products, arithmetic and copies ran while one was open for 0% of the time, Pallas kernels for 0%

commit v1 on v0

v1 whole, which is shorter than its diff:
```python
import functools

import jax
import jax.numpy as jnp
from jax import lax
from jax.experimental import pallas as pl
from jax.experimental.pallas import tpu as pltpu
from jax.sharding import PartitionSpec as P

F32 = jnp.float32
BF16 = jnp.bfloat16
LANES = 128
MESH = pl.DeviceIdType.MESH


def split2(x):
    high = x.astype(BF16)
    return high, (x - high.astype(F32)).astype(BF16)


def mm(a, b):
    return jnp.dot(a, b, preferred_element_type=F32)


def mm_t(a, b):
    return lax.dot_general(a, b, (((1,), (1,)), ((), ())), preferred_element_type=F32)


def kernel(
    n, folded, groups_of_rows,
    ts_ref, gains_ref, bounds_ref, band_ref, taps_ref, wafer_ref, modes_ref,
    out_ref,
    own_ref, xh_ref, xm_ref, y_ref,
    a_ref, b_ref, p_ref, t_ref, sib_ref, got_ref, ssq_ref,
    sib_send, sib_recv, ring_send, ring_recv,
    psend, precv, tsend, trecv, qsend, qrecv,
):
    rows, samples = ts_ref.shape
    half = samples // 2
    chips = n // 2
    hops = chips // 2
    blocks = samples // LANES
    part = rows // groups_of_rows
    bands, taps = taps_ref.shape
    wafers = modes_ref.shape[0]

    me = lax.axis_index("det")
    core = lax.rem(me, 2)
    chip = me // 2
    if folded:
        odd = lax.rem(chip, 2)
        ring = (1 - odd) * (chip // 2) + odd * (chips - 1 - chip // 2)
    else:
        ring = chip

    def chip_at(pos):
        pos = lax.rem(pos + 2 * chips, chips)
        if not folded:
            return pos
        late = pos // (chips // 2)
        return (1 - late) * 2 * pos + late * (2 * (chips - 1 - pos) + 1)

    step = 1 - 2 * core

    barrier = pltpu.get_barrier_semaphore()

    def greet(i, carry):
        pl.semaphore_signal(
            barrier, inc=1, device_id={"det": lax.rem(me + i, n)}, device_id_type=MESH
        )
        return carry

    lax.fori_loop(1, n, greet, 0)

    depth = LANES + taps
    lag = (
        lax.broadcasted_iota(jnp.int32, (depth, LANES), 1)
        + taps
        - lax.broadcasted_iota(jnp.int32, (depth, LANES), 0)
    )
    mats = []
    for band in range(bands):
        mat = jnp.zeros((depth, LANES), F32)
        for k in range(taps):
            mat = jnp.where(lag == k, taps_ref[band, k], mat)
        mats.append(jnp.concatenate([jnp.zeros((LANES - taps, LANES), F32), mat], axis=0))
    toep_h, toep_m = split2(jnp.concatenate(mats, axis=1))

    eye = lax.broadcasted_iota(jnp.int32, (rows, rows), 0) == lax.broadcasted_iota(
        jnp.int32, (rows, rows), 1
    )

    def column(ref):
        return jnp.sum(jnp.where(eye, ref[...].astype(F32), 0.0), axis=1, keepdims=True)

    band_col = column(band_ref)
    wafer_col = column(wafer_ref)

    modes = modes_ref[...]
    m1 = modes.astype(BF16).astype(F32)
    m2 = (modes - m1).astype(BF16).astype(F32)
    m3 = modes - m1 - m2
    stack = jnp.concatenate([m1, m2, m3], axis=0).astype(BF16)
    which = lax.rem(lax.broadcasted_iota(jnp.int32, (rows, 3 * wafers), 1), wafers)
    onehot = jnp.where(which.astype(F32) == wafer_col, 1.0, 0.0).astype(BF16)
    own_ref[...] = mm(onehot, stack)

    def ring_copy(d, g, who):
        span = pl.ds(g * part, part)
        src = a_ref.at[who, span] if d == 0 else b_ref.at[d - 1, who, span]
        return pltpu.make_async_remote_copy(
            src_ref=src,
            dst_ref=b_ref.at[d, who, span],
            send_sem=ring_send.at[d, who, g],
            recv_sem=ring_recv.at[d, who, g],
            device_id={"det": 2 * chip_at(ring + step) + core},
            device_id_type=MESH,
        )

    def sib_copy(g):
        span = pl.ds(g * part, part)
        return pltpu.make_async_remote_copy(
            src_ref=a_ref.at[2, span],
            dst_ref=a_ref.at[core, span],
            send_sem=sib_send.at[g],
            recv_sem=sib_recv.at[g],
            device_id={"det": 2 * chip + 1 - core},
            device_id_type=MESH,
        )

    def sib_arrival(g):
        span = pl.ds(g * part, part)
        return pltpu.make_async_remote_copy(
            src_ref=a_ref.at[2, span],
            dst_ref=a_ref.at[1 - core, span],
            send_sem=sib_send.at[g],
            recv_sem=sib_recv.at[g],
            device_id={"det": 2 * chip + 1 - core},
            device_id_type=MESH,
        )

    power = jnp.zeros((8, LANES), F32)
    sends = []
    for g in range(groups_of_rows):
        lo, hi = g * part, (g + 1) * part
        bound = [bounds_ref[lo:hi, c : c + 1] for c in range(bounds_ref.shape[1])]
        gain = [gains_ref[lo:hi, c : c + 1] for c in range(gains_ref.shape[1])]
        in_band = [band_col[lo:hi] == float(band) for band in range(bands)]
        xh_ref[0:part, 0:LANES] = jnp.zeros((part, LANES), BF16)
        xm_ref[0:part, 0:LANES] = jnp.zeros((part, LANES), BF16)
        for blk in range(blocks):
            when = lax.broadcasted_iota(jnp.int32, (part, LANES), 1) + blk * LANES
            prof = jnp.broadcast_to(gain[0], (part, LANES))
            for c, edge in enumerate(bound):
                prof = jnp.where(when >= edge, gain[c + 1], prof)
            xh, xm = split2(ts_ref[lo:hi, blk * LANES : (blk + 1) * LANES] * prof)
            at = blk * part
            xh_ref[at : at + part, LANES:] = xh
            xm_ref[at : at + part, LANES:] = xm
            if blk + 1 < blocks:
                xh_ref[at + part : at + 2 * part, 0:LANES] = xh
                xm_ref[at + part : at + 2 * part, 0:LANES] = xm
        y_ref[...] = mm(xh_ref[...], toep_h) + (
            mm(xh_ref[...], toep_m) + mm(xm_ref[...], toep_h)
        )
        cross = jnp.zeros((part, LANES), F32)
        norm = jnp.zeros((part, LANES), F32)
        for blk in range(blocks):
            at = blk * part
            filt = y_ref[at : at + part, 0:LANES]
            for band in range(1, bands):
                filt = jnp.where(
                    in_band[band], y_ref[at : at + part, band * LANES : (band + 1) * LANES], filt
                )
            y_ref[at : at + part, 0:LANES] = filt
            mode = own_ref[lo:hi, blk * LANES : (blk + 1) * LANES]
            cross = cross + filt * mode
            norm = norm + mode * mode
        coupling = (jnp.sum(cross, axis=1, keepdims=True) / samples) / (
            jnp.sum(norm, axis=1, keepdims=True) / samples + 1e-06
        )
        sq = jnp.zeros((part, LANES), F32)
        for blk in range(blocks):
            at = blk * part
            second = blk >= blocks // 2
            slot = (2 - core) if second else 2 * core
            mode = own_ref[lo:hi, blk * LANES : (blk + 1) * LANES]
            clean = (y_ref[at : at + part, 0:LANES] - coupling * mode).astype(BF16)
            col = blk * LANES - (half if second else 0)
            a_ref[slot, lo:hi, col : col + LANES] = clean
            wide = clean.astype(F32)
            sq = sq + wide * wide
        for i in range(part // 8):
            power = power + sq[8 * i : 8 * i + 8]
        if g == 0:
            pl.semaphore_wait(barrier, n - 1)
        sib = sib_copy(g)
        sib.start()
        first = ring_copy(0, g, core)
        first.start()
        sends += [sib, first]

    for g in range(groups_of_rows):
        sib_arrival(g).wait_recv()
        second = ring_copy(0, g, 1 - core)
        second.start()
        sends.append(second)

    ssq_ref[0] = power

    def power_copy(i):
        return pltpu.make_async_remote_copy(
            src_ref=ssq_ref.at[0],
            dst_ref=ssq_ref.at[i],
            send_sem=qsend.at[i],
            recv_sem=qrecv.at[i],
            device_id={"det": lax.rem(me + i, n)},
            device_id_type=MESH,
        )

    def power_start(i, carry):
        power_copy(i).start()
        return carry

    def power_wait(i, carry):
        power_copy(i).wait()
        return carry

    lax.fori_loop(1, n, power_start, 0)

    def give_sibling(d):
        return pltpu.make_async_remote_copy(
            src_ref=p_ref.at[d, 1 - core],
            dst_ref=sib_ref.at[d],
            send_sem=psend.at[d],
            recv_sem=precv.at[d],
            device_id={"det": 2 * chip + 1 - core},
            device_id_type=MESH,
        )

    def give_turned(d, to):
        return pltpu.make_async_remote_copy(
            src_ref=t_ref.at[d - 1, to],
            dst_ref=got_ref.at[core, d - 1],
            send_sem=tsend.at[d - 1, to],
            recv_sem=trecv.at[core, d - 1],
            device_id={"det": 2 * chip_at(ring - step * d) + to},
            device_id_type=MESH,
        )

    def take_turned(who, d):
        return pltpu.make_async_remote_copy(
            src_ref=t_ref.at[d - 1, 0],
            dst_ref=got_ref.at[who, d - 1],
            send_sem=tsend.at[d - 1, 0],
            recv_sem=trecv.at[who, d - 1],
            device_id={"det": 2 * chip + 1 - core},
            device_id_type=MESH,
        )

    mine = a_ref[0:2].reshape(2 * rows, half)

    def product(d):
        block = mine if d == 0 else b_ref[d - 1].reshape(2 * rows, half)
        prod = mm_t(mine, block)
        p_ref[d, 0] = prod[0:rows]
        p_ref[d, 1] = prod[rows:]
        give = give_sibling(d)
        give.start()
        sends.append(give)
        if 0 < d < hops:
            turned = prod.T
            t_ref[d - 1, 0] = turned[0:rows]
            t_ref[d - 1, 1] = turned[rows:]
            for to in range(2):
                give = give_turned(d, to)
                give.start()
                sends.append(give)

    product(0)
    for d in range(1, hops + 1):
        for flip in range(2):
            who = core if flip == 0 else 1 - core
            for g in range(groups_of_rows):
                ring_copy(d - 1, g, who).wait_recv()
                if d < hops:
                    onward = ring_copy(d, g, who)
                    onward.start()
                    sends.append(onward)
        product(d)

    lax.fori_loop(1, n, power_wait, 0)

    def add_power(i, total):
        return total + ssq_ref[i]

    total = jnp.sum(lax.fori_loop(1, n, add_power, power))
    mean_power = total / float(rows * n * samples)
    scale = 1.0 / (samples * jnp.full((rows, LANES), mean_power, F32))

    def put(pos, value):
        col = pl.multiple_of(chip_at(pos) * (2 * rows), 2 * rows)
        out_ref[:, pl.ds(col, 2 * rows)] = value * scale

    for d in range(hops + 1):
        give_sibling(d).wait_recv()
        if d == 0 or d == hops:
            put(ring + d, p_ref[d, core] + sib_ref[d])
        else:
            take_turned(1 - core, d).wait_recv()
            put(ring - step * d, p_ref[d, core] + got_ref[1 - core, d - 1])
            take_turned(core, d).wait_recv()
            put(ring + step * d, sib_ref[d] + got_ref[core, d - 1])

    for copy in sends:
        copy.wait_send()


def on_device(
    n, folded, timestream, seg_gains, seg_bounds, det_band, band_taps, det_wafer, wafer_modes
):
    rows, samples = timestream.shape
    half = samples // 2
    hops = n // 4
    pieces = 2
    part = rows // pieces
    bands = band_taps.shape[0]
    vmem = pl.BlockSpec(memory_space=pltpu.VMEM)
    dma = pltpu.SemaphoreType.DMA
    return pl.pallas_call(
        functools.partial(kernel, n, folded, pieces),
        out_shape=jax.ShapeDtypeStruct((rows, rows * n), F32),
        in_specs=[vmem] * 4 + [pl.BlockSpec(memory_space=pltpu.SMEM)] + [vmem] * 2,
        out_specs=vmem,
        scratch_shapes=[
            pltpu.VMEM((rows, samples), F32),
            pltpu.VMEM((part * samples // LANES, 2 * LANES), BF16),
            pltpu.VMEM((part * samples // LANES, 2 * LANES), BF16),
            pltpu.VMEM((part * samples // LANES, bands * LANES), F32),
            pltpu.VMEM((3, rows, half), BF16),
            pltpu.VMEM((hops, 2, rows, half), BF16),
            pltpu.VMEM((hops + 1, 2, rows, 2 * rows), F32),
            pltpu.VMEM((hops - 1, 2, rows, 2 * rows), F32),
            pltpu.VMEM((hops + 1, rows, 2 * rows), F32),
            pltpu.VMEM((2, hops - 1, rows, 2 * rows), F32),
            pltpu.VMEM((n, 8, LANES), F32),
            dma((pieces,)),
            dma((pieces,)),
            dma((hops, 2, pieces)),
            dma((hops, 2, pieces)),
            dma((hops + 1,)),
            dma((hops + 1,)),
            dma((hops - 1, 2)),
            dma((2, hops - 1)),
            dma((n,)),
            dma((n,)),
        ],
        compiler_params=pltpu.CompilerParams(
            collective_id=0, has_side_effects=True, vmem_limit_bytes=48 * 1024 * 1024
        ),
    )(
        timestream,
        seg_gains,
        seg_bounds,
        det_band.reshape(1, rows),
        band_taps,
        det_wafer.reshape(1, rows),
        wafer_modes,
    )


def solution(mesh):
    n = mesh.shape["det"]
    folded = mesh.shape["groups"] == 2
    return jax.shard_map(
        functools.partial(on_device, n, folded),
        mesh=mesh,
        in_specs=(
            P(("groups", "det"), None),
            P(("groups", "det"), None),
            P(("groups", "det"), None),
            P(("groups", "det")),
            P(),
            P(("groups", "det")),
            P("groups", None),
        ),
        out_specs=P(("groups", "det"), None),
        check_vma=False,
    )
```

time: 121 us -> 42.2 us (0.35)
  waiting for transfers between devices: 41.1 us -> 0 us
  Pallas kernels: 0 us -> 37.1 us
  blocking collectives: 36.2 us -> 0 us
  matrix products: 15.9 us -> 0 us
  between operations: 14.1 us -> 0.02 us
  other arithmetic: 4.54 us -> 0 us
  local copies, waits for them, and re-layouts: 8.31 us -> 4.88 us
    all_gather x1 -> x0, waiting for transfers between devices: 41.1 us -> none  [on_device(): lax.all_gather(cleaned, 'det', axis=0, tiled=True)]
    pallas_call x0 -> x1, Pallas kernels: none -> 37.1 us  [on_device(): pl.pallas_call(functools.partial(kernel, n, folded, pieces), out_shape=ja...]
    psum x1 -> x0, blocking collectives: 36.2 us -> none  [on_device(): lax.psum(jnp.sum(widened * widened), 'det') / (det_rows * devices * samples)]
    conv_general_dilated x1 -> x0, matrix products: 8.17 us -> none  [filter_rows(): lax.conv_general_dilated(padded[None], kernel, (1,), 'VALID', dimension_n...]
    dot_general x2 -> x0, matrix products: 7.73 us -> none  [the longest x1 6.93 us: pair_block(): lax.dot_general(left_rows, right_rows, (((1,), (1,)), ((), ())), preferre...]
    conv_general_dilated x5 -> x0, local copies, waits for them, and re-layouts: 4.88 us -> none  [filter_rows(): lax.conv_general_dilated(padded[None], kernel, (1,), 'VALID', dimension_n...]
    unnamed x4 -> x17, local copies, waits for them, and re-layouts: 0.01 us -> 4.88 us
    mul x1 -> x0, other arithmetic: 2.1 us -> none  [filter_rows(): scaled = timestream * profile]
  transfers between devices with their start and end apart: 1 -> 0, of which waited for: 1 -> 0; matrix products, arithmetic and copies ran while one was open for 0% -> 0% of each run, Pallas kernels for 0% -> 0%
where the time goes in v1:
time: 42.2 us; the launch traced here: 42 us
  Pallas kernels  37.1 us (88%)
  local copies, waits for them, and re-layouts  4.88 us (12%)
    pallas_call x1, Pallas kernels, on_device(): pl.pallas_call(functools.partial(kernel, n, folded, pieces), out_shape=ja...  37.1 us
    unnamed x17, local copies, waits for them, and re-layouts  4.88 us

profile of v1, /device:TPU:0, one launch (start us, length us, event | category | flops | bytes accessed | tf_op | source)
XLA Modules:
  0.0 42.0 jit_solution(3637993086915463838)
XLA Ops:
  0.0 0.0 copy-start.5
  0.0 0.7 %copy-done.5 = f32[64,4]{0,1:T(4,128)S(1)} copy-done((f32[64,4]{0,1:T(4,128)S(1)}, f32[64,4]{0,1:T(4,128)}, u32[]{:S(2)}) %copy-start.5) | copy-done | bytes 1048
  0.7 0.0 copy-start.6
  0.7 0.1 copy.8.gains_ref
  0.8 0.6 %copy-done.6 = s32[64,3]{0,1:T(4,128)S(1)} copy-done((s32[64,3]{0,1:T(4,128)S(1)}, s32[64,3]{0,1:T(4,128)}, u32[]{:S(2)}) %copy-start.6) | copy-done | bytes 792
  1.4 0.0 copy-start.2
  1.4 0.0 copy-start.3
  1.4 0.0 copy-start.4
  1.4 0.1 copy.9.bounds_ref
  1.5 0.6 %copy-done.2 = f32[2,32]{1,0:T(2,128)S(1)} copy-done((f32[2,32]{1,0:T(2,128)S(1)}, f32[2,32]{1,0:T(2,128)}, u32[]{:S(2)}) %copy-start.2) | copy-done | bytes 280
  2.0 0.0 copy-done.3
  2.0 0.0 copy-done.4
  2.1 0.0 copy-start
  2.1 1.2 %copy-done = f32[64,4096]{1,0:T(8,128)S(1)} copy-done((f32[64,4096]{1,0:T(8,128)S(1)}, f32[64,4096]{1,0:T(8,128)}, u32[]{:S(2)}) %copy-start) | copy-done | bytes 1048600
  3.3 0.0 copy-start.1
  3.3 0.9 %copy-done.1 = f32[8,4096]{1,0:T(8,128)S(1)} copy-done((f32[8,4096]{1,0:T(8,128)S(1)}, f32[8,4096]{1,0:T(8,128)}, u32[]{:S(2)}) %copy-start.1) | copy-done | bytes 131096
  4.2 37.1 %shard_map.73 = f32[64,1024]{1,0:T(8,128)S(1)} custom-call(f32[64,4096]{1,0:T(8,128)S(1)} %copy-done, f32[64,4]{1,0:T(8,128)S(1)} %copy.8.gains_ref, s32[64,3]{1,0:T(8,128)S(1)} %copy.9.bounds_ref, s32[1,64]{1,0:T(1,128)S(1)} %bitcast.2, f32[2,32]{1,0:T(2,128)S(1)} %copy-done.2, s32[1,64]{1,0:T(1,128)S(1)} %bitcast.3, f32[8,4096]{1,0:T(8,128)S(1)} %copy-done.1), custom_call_target="tpu_custom_call" | custom-call | tf_op jit(solution)/shard_map/pallas_call | solution.py:330
  41.3 0.7 %copy.11 = f32[64,1024]{1,0:T(8,128)} copy(f32[64,1024]{1,0:T(8,128)S(1)} %shard_map.73) | data formatting | bytes 524288
Async XLA Ops:
  0.0 0.7 %copy-start.5 = (f32[64,4]{0,1:T(4,128)S(1)}, f32[64,4]{0,1:T(4,128)}, u32[]{:S(2)}) copy-start(f32[64,4]{0,1:T(4,128)} %param.8) | copy-start | bytes 3076
  0.7 0.7 %copy-start.6 = (s32[64,3]{0,1:T(4,128)S(1)}, s32[64,3]{0,1:T(4,128)}, u32[]{:S(2)}) copy-start(s32[64,3]{0,1:T(4,128)} %param.9) | copy-start | bytes 2308
  1.4 0.7 %copy-start.2 = (f32[2,32]{1,0:T(2,128)S(1)}, f32[2,32]{1,0:T(2,128)}, u32[]{:S(2)}) copy-start(f32[2,32]{1,0:T(2,128)} %taps_ref.1) | copy-start | bytes 772
  1.4 0.7 %copy-start.3 = (s32[64]{0:T(128)S(1)}, s32[64]{0:T(128)}, u32[]{:S(2)}) copy-start(s32[64]{0:T(128)} %param.10) | copy-start | bytes 772
  1.4 0.7 %copy-start.4 = (s32[64]{0:T(128)S(1)}, s32[64]{0:T(128)}, u32[]{:S(2)}) copy-start(s32[64]{0:T(128)} %param.12) | copy-start | bytes 772
  2.1 1.2 %copy-start = (f32[64,4096]{1,0:T(8,128)S(1)}, f32[64,4096]{1,0:T(8,128)}, u32[]{:S(2)}) copy-start(f32[64,4096]{1,0:T(8,128)} %ts_ref.1) | copy-start | bytes 3145732
  3.3 0.9 %copy-start.1 = (f32[8,4096]{1,0:T(8,128)S(1)}, f32[8,4096]{1,0:T(8,128)}, u32[]{:S(2)}) copy-start(f32[8,4096]{1,0:T(8,128)} %modes_ref.1) | copy-start | bytes 393220

commit v2 on v1

--- a/solution.py
+++ b/solution.py
@@ -28,14 +28,15 @@
 
 def kernel(
     n, folded, groups_of_rows,
-    ts_ref, gains_ref, bounds_ref, band_ref, taps_ref, wafer_ref, modes_ref,
+    ts_hbm, gains_hbm, bounds_hbm, band_hbm, taps_hbm, wafer_hbm, modes_hbm,
     out_ref,
+    ts_ref, gains_ref, bounds_ref, band_ref, taps_ref, wafer_ref, modes_ref, in_sem,
     own_ref, xh_ref, xm_ref, y_ref,
     a_ref, b_ref, p_ref, t_ref, sib_ref, got_ref, ssq_ref,
     sib_send, sib_recv, ring_send, ring_recv,
     psend, precv, tsend, trecv, qsend, qrecv,
 ):
-    rows, samples = ts_ref.shape
+    rows, samples = ts_hbm.shape
     half = samples // 2
     chips = n // 2
     hops = chips // 2
@@ -71,6 +72,31 @@
         return carry
 
     lax.fori_loop(1, n, greet, 0)
+
+    small = [
+        pltpu.make_async_copy(src, dst, in_sem.at[i])
+        for i, (src, dst) in enumerate(
+            (
+                (taps_hbm, taps_ref),
+                (modes_hbm, modes_ref),
+                (band_hbm, band_ref),
+                (wafer_hbm, wafer_ref),
+                (gains_hbm, gains_ref),
+                (bounds_hbm, bounds_ref),
+            )
+        )
+    ]
+    large = [
+        pltpu.make_async_copy(
+            ts_hbm.at[pl.ds(g * part, part)],
+            ts_ref.at[pl.ds(g * part, part)],
+            in_sem.at[len(small) + g],
+        )
+        for g in range(groups_of_rows)
+    ]
+    for copy in small + large:
+        copy.start()
+    small[0].wait()
 
     depth = LANES + taps
     lag = (
@@ -86,15 +112,21 @@
         mats.append(jnp.concatenate([jnp.zeros((LANES - taps, LANES), F32), mat], axis=0))
     toep_h, toep_m = split2(jnp.concatenate(mats, axis=1))
 
+    for copy in small[1:]:
+        copy.wait()
+
     eye = lax.broadcasted_iota(jnp.int32, (rows, rows), 0) == lax.broadcasted_iota(
         jnp.int32, (rows, rows), 1
     )
 
-    def column(ref):
-        return jnp.sum(jnp.where(eye, ref[...].astype(F32), 0.0), axis=1, keepdims=True)
+    def column(ref, i=0):
+        row = ref[i : i + 1, :].astype(F32)
+        return jnp.sum(jnp.where(eye, row, 0.0), axis=1, keepdims=True)
 
     band_col = column(band_ref)
     wafer_col = column(wafer_ref)
+    gain_cols = [column(gains_ref, i) for i in range(gains_ref.shape[0])]
+    bound_cols = [column(bounds_ref, i).astype(jnp.int32) for i in range(bounds_ref.shape[0])]
 
     modes = modes_ref[...]
     m1 = modes.astype(BF16).astype(F32)
@@ -143,9 +175,10 @@
     sends = []
     for g in range(groups_of_rows):
         lo, hi = g * part, (g + 1) * part
-        bound = [bounds_ref[lo:hi, c : c + 1] for c in range(bounds_ref.shape[1])]
-        gain = [gains_ref[lo:hi, c : c + 1] for c in range(gains_ref.shape[1])]
+        bound = [col[lo:hi] for col in bound_cols]
+        gain = [col[lo:hi] for col in gain_cols]
         in_band = [band_col[lo:hi] == float(band) for band in range(bands)]
+        large[g].wait()
         xh_ref[0:part, 0:LANES] = jnp.zeros((part, LANES), BF16)
         xm_ref[0:part, 0:LANES] = jnp.zeros((part, LANES), BF16)
         for blk in range(blocks):
@@ -325,14 +358,22 @@
     pieces = 2
     part = rows // pieces
     bands = band_taps.shape[0]
-    vmem = pl.BlockSpec(memory_space=pltpu.VMEM)
+    hbm = pl.BlockSpec(memory_space=pltpu.HBM)
     dma = pltpu.SemaphoreType.DMA
     return pl.pallas_call(
         functools.partial(kernel, n, folded, pieces),
         out_shape=jax.ShapeDtypeStruct((rows, rows * n), F32),
-        in_specs=[vmem] * 4 + [pl.BlockSpec(memory_space=pltpu.SMEM)] + [vmem] * 2,
-        out_specs=vmem,
+        in_specs=[hbm] * 7,
+        out_specs=pl.BlockSpec(memory_space=pltpu.VMEM),
         scratch_shapes=[
+            pltpu.VMEM((rows, samples), F32),
+            pltpu.VMEM(seg_gains.shape[::-1], F32),
+            pltpu.VMEM(seg_bounds.shape[::-1], jnp.int32),
+            pltpu.VMEM((1, rows), jnp.int32),
+            pltpu.SMEM(band_taps.shape, F32),
+            pltpu.VMEM((1, rows), jnp.int32),
+            pltpu.VMEM(wafer_modes.shape, F32),
+            dma((6 + pieces,)),
             pltpu.VMEM((rows, samples), F32),
             pltpu.VMEM((part * samples // LANES, 2 * LANES), BF16),
             pltpu.VMEM((part * samples // LANES, 2 * LANES), BF16),
@@ -356,12 +397,12 @@
             dma((n,)),
         ],
         compiler_params=pltpu.CompilerParams(
-            collective_id=0, has_side_effects=True, vmem_limit_bytes=48 * 1024 * 1024
+            collective_id=0, has_side_effects=True, vmem_limit_bytes=63 * 1024 * 1024
         ),
     )(
         timestream,
-        seg_gains,
-        seg_bounds,
+        seg_gains.T,
+        seg_bounds.T,
         det_band.reshape(1, rows),
         band_taps,
         det_wafer.reshape(1, rows),

time: 42.2 us -> 39 us (0.924)
  local copies, waits for them, and re-layouts: 4.88 us -> 1.67 us
    unnamed x17 -> x1, local copies, waits for them, and re-layouts: 4.88 us -> 1.67 us
where the time goes in v2:
time: 39 us; the launch traced here: 38.8 us
  Pallas kernels  37.2 us (95%)
  local copies, waits for them, and re-layouts  1.67 us (4%)
    pallas_call x1, Pallas kernels, on_device(): pl.pallas_call(functools.partial(kernel, n, folded, pieces), out_shape=ja...  37.2 us
    unnamed x1, local copies, waits for them, and re-layouts  1.67 us

profile of v2, /device:TPU:0, one launch (start us, length us, event | category | flops | bytes accessed | tf_op | source)
XLA Modules:
  0.0 38.8 jit_solution(17942881788765740542)
XLA Ops:
  0.0 37.2 %shard_map.73 = f32[64,1024]{1,0:T(8,128)} custom-call(f32[64,4096]{1,0:T(8,128)} %ts_hbm.1, f32[4,64]{1,0:T(4,128)} %bitcast.4, s32[3,64]{1,0:T(4,128)} %bitcast.5, s32[1,64]{1,0:T(1,128)} %bitcast.6, f32[2,32]{1,0:T(2,128)} %taps_hbm.1, s32[1,64]{1,0:T(1,128)} %bitcast.7, f32[8,4096]{1,0:T(8,128)} %modes_hbm.1), custom_call_target="tpu_custom_call" | custom-call | tf_op jit(solution)/shard_map/pallas_call | solution.py:363
  37.2 1.7 %copy.9 = f32[64,1024]{1,0:T(8,128)} copy(f32[64,1024]{1,0:T(8,128)} %shard_map.73) | data formatting | bytes 524288

commit v3 on v2

--- a/solution.py
+++ b/solution.py
@@ -29,7 +29,7 @@
 def kernel(
     n, folded, groups_of_rows,
     ts_hbm, gains_hbm, bounds_hbm, band_hbm, taps_hbm, wafer_hbm, modes_hbm,
-    out_ref,
+    out_ref, power_ref,
     ts_ref, gains_ref, bounds_ref, band_ref, taps_ref, wafer_ref, modes_ref, in_sem,
     own_ref, xh_ref, xm_ref, y_ref,
     a_ref, b_ref, p_ref, t_ref, sib_ref, got_ref, ssq_ref,
@@ -65,13 +65,12 @@
 
     barrier = pltpu.get_barrier_semaphore()
 
-    def greet(i, carry):
-        pl.semaphore_signal(
-            barrier, inc=1, device_id={"det": lax.rem(me + i, n)}, device_id_type=MESH
-        )
-        return carry
-
-    lax.fori_loop(1, n, greet, 0)
+    for near in (
+        2 * chip + 1 - core,
+        2 * chip_at(ring + 1) + core,
+        2 * chip_at(ring - 1) + core,
+    ):
+        pl.semaphore_signal(barrier, inc=1, device_id={"det": near}, device_id_type=MESH)
 
     small = [
         pltpu.make_async_copy(src, dst, in_sem.at[i])
@@ -226,7 +225,7 @@
         for i in range(part // 8):
             power = power + sq[8 * i : 8 * i + 8]
         if g == 0:
-            pl.semaphore_wait(barrier, n - 1)
+            pl.semaphore_wait(barrier, 3)
         sib = sib_copy(g)
         sib.start()
         first = ring_copy(0, g, core)
@@ -239,27 +238,30 @@
         second.start()
         sends.append(second)
 
-    ssq_ref[0] = power
-
-    def power_copy(i):
-        return pltpu.make_async_remote_copy(
-            src_ref=ssq_ref.at[0],
-            dst_ref=ssq_ref.at[i],
+    def swap_power(src, dst, i):
+        return pltpu.make_async_remote_copy(
+            src_ref=ssq_ref.at[src],
+            dst_ref=ssq_ref.at[dst],
             send_sem=qsend.at[i],
             recv_sem=qrecv.at[i],
-            device_id={"det": lax.rem(me + i, n)},
-            device_id_type=MESH,
-        )
-
-    def power_start(i, carry):
-        power_copy(i).start()
-        return carry
-
-    def power_wait(i, carry):
-        power_copy(i).wait()
-        return carry
-
-    lax.fori_loop(1, n, power_start, 0)
+            device_id={"det": 2 * chip + 1 - core},
+            device_id_type=MESH,
+        )
+
+    def pass_power(d):
+        return pltpu.make_async_remote_copy(
+            src_ref=ssq_ref.at[d],
+            dst_ref=ssq_ref.at[d + 1],
+            send_sem=qsend.at[2 + d],
+            recv_sem=qrecv.at[2 + d],
+            device_id={"det": 2 * chip_at(ring + step) + core},
+            device_id_type=MESH,
+        )
+
+    ssq_ref[hops + 1] = power
+    swap_first = swap_power(hops + 1, hops + 2, 0)
+    swap_first.start()
+    sends.append(swap_first)
 
     def give_sibling(d):
         return pltpu.make_async_remote_copy(
@@ -311,6 +313,12 @@
                 sends.append(give)
 
     product(0)
+    swap_first.wait_recv()
+    ssq_ref[0] = power + ssq_ref[hops + 2]
+    onward = pass_power(0)
+    onward.start()
+    sends.append(onward)
+    beside = jnp.zeros((8, LANES), F32)
     for d in range(1, hops + 1):
         for flip in range(2):
             who = core if flip == 0 else 1 - core
@@ -320,20 +328,27 @@
                     onward = ring_copy(d, g, who)
                     onward.start()
                     sends.append(onward)
+        pass_power(d - 1).wait_recv()
+        if d < hops:
+            onward = pass_power(d)
+            onward.start()
+            sends.append(onward)
+            beside = beside + ssq_ref[d]
+        if d == hops - 1:
+            ssq_ref[hops + 3] = beside
+            swap_last = swap_power(hops + 3, hops + 4, 1)
+            swap_last.start()
+            sends.append(swap_last)
         product(d)
 
-    lax.fori_loop(1, n, power_wait, 0)
-
-    def add_power(i, total):
-        return total + ssq_ref[i]
-
-    total = jnp.sum(lax.fori_loop(1, n, add_power, power))
+    swap_last.wait_recv()
+    total = jnp.sum(ssq_ref[0] + beside + ssq_ref[hops + 4] + ssq_ref[hops])
     mean_power = total / float(rows * n * samples)
-    scale = 1.0 / (samples * jnp.full((rows, LANES), mean_power, F32))
+    power_ref[...] = jnp.full((8, LANES), mean_power, F32)
 
     def put(pos, value):
         col = pl.multiple_of(chip_at(pos) * (2 * rows), 2 * rows)
-        out_ref[:, pl.ds(col, 2 * rows)] = value * scale
+        out_ref[:, pl.ds(col, 2 * rows)] = value
 
     for d in range(hops + 1):
         give_sibling(d).wait_recv()
@@ -360,11 +375,14 @@
     bands = band_taps.shape[0]
     hbm = pl.BlockSpec(memory_space=pltpu.HBM)
     dma = pltpu.SemaphoreType.DMA
-    return pl.pallas_call(
+    gram, mean_power = pl.pallas_call(
         functools.partial(kernel, n, folded, pieces),
-        out_shape=jax.ShapeDtypeStruct((rows, rows * n), F32),
+        out_shape=(
+            jax.ShapeDtypeStruct((rows, rows * n), F32),
+            jax.ShapeDtypeStruct((8, LANES), F32),
+        ),
         in_specs=[hbm] * 7,
-        out_specs=pl.BlockSpec(memory_space=pltpu.VMEM),
+        out_specs=(pl.BlockSpec(memory_space=pltpu.VMEM),) * 2,
         scratch_shapes=[
             pltpu.VMEM((rows, samples), F32),
             pltpu.VMEM(seg_gains.shape[::-1], F32),
@@ -384,7 +402,7 @@
             pltpu.VMEM((hops - 1, 2, rows, 2 * rows), F32),
             pltpu.VMEM((hops + 1, rows, 2 * rows), F32),
             pltpu.VMEM((2, hops - 1, rows, 2 * rows), F32),
-            pltpu.VMEM((n, 8, LANES), F32),
+            pltpu.VMEM((hops + 5, 8, LANES), F32),
             dma((pieces,)),
             dma((pieces,)),
             dma((hops, 2, pieces)),
@@ -393,8 +411,8 @@
             dma((hops + 1,)),
             dma((hops - 1, 2)),
             dma((2, hops - 1)),
-            dma((n,)),
-            dma((n,)),
+            dma((hops + 2,)),
+            dma((hops + 2,)),
         ],
         compiler_params=pltpu.CompilerParams(
             collective_id=0, has_side_effects=True, vmem_limit_bytes=63 * 1024 * 1024
@@ -408,6 +426,7 @@
         det_wafer.reshape(1, rows),
         wafer_modes,
     )
+    return gram / (samples * mean_power[0, 0])
 
 
 def solution(mesh):

time: 39 us -> 38.9 us (level); the launches traced: 38.8 us -> 38.2 us
  Pallas kernels: 37.2 us -> 34.7 us
  other arithmetic: 0 us -> 1.68 us
  between operations: 0.01 us -> 0.66 us
  local copies, waits for them, and re-layouts: 1.67 us -> 1.2 us
    pallas_call x1, Pallas kernels: 37.2 us -> 34.7 us  [on_device(): pl.pallas_call(functools.partial(kernel, n, folded, pieces), out_shape=(j...]
    div x0 -> x1, other arithmetic: none -> 1.68 us  [on_device(): return gram / (samples * mean_power[0, 0])]
    unnamed x1 -> x0, local copies, waits for them, and re-layouts: 1.67 us -> none
    slice x0 -> x1, local copies, waits for them, and re-layouts: none -> 1.2 us  [on_device(): return gram / (samples * mean_power[0, 0])]
where the time goes in v3:
time: 38.9 us; the launch traced here: 38.2 us
  Pallas kernels  34.7 us (89%)
  other arithmetic  1.68 us (4%)
  local copies, waits for them, and re-layouts  1.2 us (3%)
  between operations  0.66 us (2%)
    pallas_call x1, Pallas kernels, on_device(): pl.pallas_call(functools.partial(kernel, n, folded, pieces), out_shape=(j...  34.7 us
    div x1, other arithmetic, on_device(): return gram / (samples * mean_power[0, 0])  1.68 us
    slice x1, local copies, waits for them, and re-layouts, on_device(): return gram / (samples * mean_power[0, 0])  1.2 us

profile of v3, /device:TPU:0, one launch (start us, length us, event | category | flops | bytes accessed | tf_op | source)
XLA Modules:
  0.0 38.2 jit_solution(15685451055776784282)
XLA Ops:
  0.0 34.7 %shard_map.73 = (f32[64,1024]{1,0:T(8,128)}, f32[8,128]{1,0:T(8,128)}) custom-call(f32[64,4096]{1,0:T(8,128)} %ts_hbm.1, f32[4,64]{1,0:T(4,128)} %bitcast.5, s32[3,64]{1,0:T(4,128)} %bitcast.6, s32[1,64]{1,0:T(1,128)} %bitcast.7, f32[2,32]{1,0:T(2,128)} %taps_hbm.1, s32[1,64]{1,0:T(1,128)} %bitcast.8, f32[8,4096]{1,0:T(8,128)} %modes_hbm.1), custom_call_target="tpu_custom_call" | custom-call | tf_op jit(solution)/shard_map/pallas_call | solution.py:378
  34.7 1.2 %slice.3 = f32[1,1]{1,0:T(1,128)} slice(f32[8,128]{1,0:T(8,128)} %get-tuple-element.8), slice={[0:1], [0:1]} | slice | bytes 8 | tf_op jit(solution)/shard_map/slice | solution.py:429
  36.5 1.7 %broadcast_divide_fusion = f32[64,1024]{1,0:T(8,128)} fusion(f32[64,1024]{1,0:T(8,128)} %get-tuple-element.7, f32[]{:T(128)} %bitcast.4), kind=kLoop, calls=%fused_computation | loop fusion | flops 65536 | bytes 524292 | tf_op jit(solution)/shard_map/div | solution.py:429

commit v4 on v3

--- a/solution.py
+++ b/solution.py
@@ -29,7 +29,7 @@
 def kernel(
     n, folded, groups_of_rows,
     ts_hbm, gains_hbm, bounds_hbm, band_hbm, taps_hbm, wafer_hbm, modes_hbm,
-    out_ref, power_ref,
+    out_ref,
     ts_ref, gains_ref, bounds_ref, band_ref, taps_ref, wafer_ref, modes_ref, in_sem,
     own_ref, xh_ref, xm_ref, y_ref,
     a_ref, b_ref, p_ref, t_ref, sib_ref, got_ref, ssq_ref,
@@ -344,11 +344,11 @@
     swap_last.wait_recv()
     total = jnp.sum(ssq_ref[0] + beside + ssq_ref[hops + 4] + ssq_ref[hops])
     mean_power = total / float(rows * n * samples)
-    power_ref[...] = jnp.full((8, LANES), mean_power, F32)
+    scale = 1.0 / (samples * jnp.full((rows, LANES), mean_power, F32))
 
     def put(pos, value):
         col = pl.multiple_of(chip_at(pos) * (2 * rows), 2 * rows)
-        out_ref[:, pl.ds(col, 2 * rows)] = value
+        out_ref[:, pl.ds(col, 2 * rows)] = value * scale
 
     for d in range(hops + 1):
         give_sibling(d).wait_recv()
@@ -375,14 +375,11 @@
     bands = band_taps.shape[0]
     hbm = pl.BlockSpec(memory_space=pltpu.HBM)
     dma = pltpu.SemaphoreType.DMA
-    gram, mean_power = pl.pallas_call(
+    return pl.pallas_call(
         functools.partial(kernel, n, folded, pieces),
-        out_shape=(
-            jax.ShapeDtypeStruct((rows, rows * n), F32),
-            jax.ShapeDtypeStruct((8, LANES), F32),
-        ),
+        out_shape=jax.ShapeDtypeStruct((rows, rows * n), F32),
         in_specs=[hbm] * 7,
-        out_specs=(pl.BlockSpec(memory_space=pltpu.VMEM),) * 2,
+        out_specs=pl.BlockSpec(memory_space=pltpu.VMEM),
         scratch_shapes=[
             pltpu.VMEM((rows, samples), F32),
             pltpu.VMEM(seg_gains.shape[::-1], F32),
@@ -426,7 +423,6 @@
         det_wafer.reshape(1, rows),
         wafer_modes,
     )
-    return gram / (samples * mean_power[0, 0])
 
 
 def solution(mesh):

time: 38.9 us -> 37 us (0.951)
  other arithmetic: 1.68 us -> 0 us
  between operations: 0.66 us -> 0.01 us
  local copies, waits for them, and re-layouts: 1.2 us -> 1.67 us
    div x1 -> x0, other arithmetic: 1.68 us -> none  [on_device(): return gram / (samples * mean_power[0, 0])]
    unnamed x0 -> x1, local copies, waits for them, and re-layouts: none -> 1.67 us
    slice x1 -> x0, local copies, waits for them, and re-layouts: 1.2 us -> none  [on_device(): return gram / (samples * mean_power[0, 0])]
where the time goes in v4:
time: 37 us; the launch traced here: 36.4 us
  Pallas kernels  34.7 us (94%)
  local copies, waits for them, and re-layouts  1.67 us (5%)
    pallas_call x1, Pallas kernels, on_device(): pl.pallas_call(functools.partial(kernel, n, folded, pieces), out_shape=ja...  34.7 us
    unnamed x1, local copies, waits for them, and re-layouts  1.67 us

profile of v4, /device:TPU:0, one launch (start us, length us, event | category | flops | bytes accessed | tf_op | source)
XLA Modules:
  0.0 36.4 jit_solution(3634057301524828782)
XLA Ops:
  0.0 34.7 %shard_map.73 = f32[64,1024]{1,0:T(8,128)} custom-call(f32[64,4096]{1,0:T(8,128)} %ts_hbm.1, f32[4,64]{1,0:T(4,128)} %bitcast.4, s32[3,64]{1,0:T(4,128)} %bitcast.5, s32[1,64]{1,0:T(1,128)} %bitcast.6, f32[2,32]{1,0:T(2,128)} %taps_hbm.1, s32[1,64]{1,0:T(1,128)} %bitcast.7, f32[8,4096]{1,0:T(8,128)} %modes_hbm.1), custom_call_target="tpu_custom_call" | custom-call | tf_op jit(solution)/shard_map/pallas_call | solution.py:378
  34.7 1.7 %copy.9 = f32[64,1024]{1,0:T(8,128)} copy(f32[64,1024]{1,0:T(8,128)} %shard_map.73) | data formatting | bytes 524288
